TPU v7x, 32 devices: a whole 2x2x4 slice. The times are simulated.
32 devices in a mesh: dp: 8 (over z, x), tensor: 4 (over y, core).
Axes of the slice: x: 2, y: 2, z: 4, core: 2. Of those that a mesh axis runs over, the one named last changes fastest.
Arguments:
- tokens: bfloat16 [96, 196, 512], P('dp'), may hold values from -6 to 6
- cotangent: bfloat16 [96, 196, 512], P('dp'), may hold values from -6 to 6
- region_ids: int32 [196], replicated, may hold values from 0 to 3
- relative_index: int32 [49, 49], replicated, may hold values from 0 to 168
- shared_vectors: float32 [6, 512], replicated, may hold values from -1.5 to 2, as said below
- input_weight: float32 [512, 1536], P(None, 'tensor'), may hold values from -0.25 to 0.25
- head_bias: float32 [2, 512], P(None, 'tensor'), may hold values from -3 to 3
- output_weight: float32 [512, 512], P('tensor'), may hold values from -0.75 to 0.75
- expand_weight: float32 [512, 2048], P(None, 'tensor'), may hold values from -0.25 to 0.25
- expand_bias: float32 [2048], P('tensor'), may hold values from -3 to 3
- reduce_weight: float32 [2048, 512], P('tensor'), may hold values from -0.1875 to 0.1875
- bias_table: float32 [169, 16], P(None, 'tensor'), may hold values from -5 to 5
- moment_shared: float32 [6, 512], replicated, may hold values from -1 to 1
- moment_input: float32 [512, 1536], P(None, 'tensor'), may hold values from -1 to 1
- moment_head: float32 [2, 512], P(None, 'tensor'), may hold values from -1 to 1
- moment_output: float32 [512, 512], P('tensor'), may hold values from -1 to 1
- moment_expand: float32 [512, 2048], P(None, 'tensor'), may hold values from -1 to 1
- moment_bias: float32 [2048], P('tensor'), may hold values from -1 to 1
- moment_reduce: float32 [2048, 512], P('tensor'), may hold values from -1 to 1
- moment_table: float32 [169, 16], P(None, 'tensor'), may hold values from -1 to 1
Outputs:
- block_out: bfloat16 [96, 196, 512], P('dp')
- input_grad: float32 [96, 196, 512], P('dp')
- grad_shared: float32 [6, 512], replicated
- grad_input: float32 [512, 1536], P('dp', 'tensor')
- grad_head: float32 [2, 512], P(None, 'tensor')
- grad_output: float32 [512, 512], P('tensor', 'dp')
- grad_expand: float32 [512, 2048], P('dp', 'tensor')
- grad_bias: float32 [2048], P('tensor')
- grad_reduce: float32 [2048, 512], P('tensor', 'dp')
- grad_table: float32 [169, 16], P(None, 'tensor')
- update_shared: float32 [6, 512], replicated
- update_input: float32 [512, 1536], P('dp', 'tensor')
- update_head: float32 [2, 512], P(None, 'tensor')
- update_output: float32 [512, 512], P('tensor', 'dp')
- update_expand: float32 [512, 2048], P('dp', 'tensor')
- update_bias: float32 [2048], P('tensor')
- update_reduce: float32 [2048, 512], P('tensor', 'dp')
- update_table: float32 [169, 16], P(None, 'tensor')
- state_shared: float32 [6, 512], replicated
- state_input: float32 [512, 1536], P('dp', 'tensor')
- state_head: float32 [2, 512], P(None, 'tensor')
- state_output: float32 [512, 512], P('tensor', 'dp')
- state_expand: float32 [512, 2048], P('dp', 'tensor')
- state_bias: float32 [2048], P('tensor')
- state_reduce: float32 [2048, 512], P('tensor', 'dp')
- state_table: float32 [169, 16], P(None, 'tensor')
Inputs may be any that keep to these rules, and one draw needn't show every extreme that they name: `shared_vectors`: rows 0 and 3 lie in 0.5 to 2.
All inputs are finite; a program needn't handle non-finite values.
Results may differ from a plain program's by a relative error of at most 0.012.
The roundings to bfloat16 on the way count: a program that leaves them out, or rounds other values in their place, can miss the bound.
Values sent between devices are 32-bit elements; how exact they have to be, the bound alone decides.
No kernel may reach another device: no remote copies, remote signals or barrier semaphores. Data moves between devices by JAX's collectives and lax.ppermute only.
A program may use at most 256 MiB of HBM per device.

v0:
```python
import math

import jax
import jax.numpy as jnp
from jax import lax
from jax.sharding import PartitionSpec as P

SIDE = 14
WIN = 7
SHIFT = 3
NS_STEPS = 5


highest = lax.Precision.HIGHEST
norm_epsilon = 1e-05
moment_decay = 0.8
matrix_rate = 1.0
vector_rate = 1.0
quintic_coef = (3.4445, -4.775, 2.0315)
masked_logit = -1e30


def spread(block, axis, source):
    block = jnp.where(lax.axis_index(axis) == source, block, jnp.zeros_like(block))
    return lax.psum(block, axis)


def layer_norm(values, gain_vector, offset):
    centred = values - jnp.mean(values, axis=-1, keepdims=True)
    variance = jnp.mean(centred * centred, axis=-1, keepdims=True)
    return centred * lax.rsqrt(variance + norm_epsilon) * gain_vector + offset


def gelu_exact(values):
    return 0.5 * values * (1.0 + lax.erf(values * (1.0 / math.sqrt(2.0))))


def roll_tokens(values, amount):
    image_grid = values.reshape(values.shape[0], SIDE, SIDE, values.shape[-1])
    return jnp.roll(image_grid, (amount, amount), axis=(1, 2)).reshape(values.shape)


def position_tables():
    position = jnp.arange(SIDE * SIDE)
    grid_row = position // SIDE
    grid_col = position % SIDE
    window = grid_row // WIN * (SIDE // WIN) + grid_col // WIN
    inside = grid_row % WIN * WIN + grid_col % WIN
    same_window = window[:, None] == window[None, :]
    placement = (inside[:, None] == jnp.arange(WIN * WIN)[None, :]).astype(jnp.float32)
    return (same_window, placement)


def index_table(relative_index, table_rows):
    return (relative_index.reshape(-1)[:, None] == jnp.arange(table_rows)[None, :]).astype(
        jnp.float32
    )


def attention_logits(queries, key_rows, bias_all, allowed):
    logits = (
        jnp.einsum("gphe,gqhe->ghpq", queries, key_rows, preferred_element_type=jnp.float32)
        + bias_all[None]
    )
    return jnp.where(allowed[None, None], logits, masked_logit)


def orthogonalize(matrix):
    tall = matrix.shape[0] > matrix.shape[1]
    iterate = matrix.T if tall else matrix
    iterate = iterate * lax.rsqrt(jnp.sum(iterate * iterate) + 1e-07)
    for step_index in range(NS_STEPS):
        gram_matrix = jnp.dot(iterate, iterate.T, precision=highest)
        polynomial = quintic_coef[1] * gram_matrix + quintic_coef[2] * jnp.dot(
            gram_matrix, gram_matrix, precision=highest
        )
        iterate = quintic_coef[0] * iterate + jnp.dot(polynomial, iterate, precision=highest)
    return iterate.T if tall else iterate


def send_back(own_piece, owner_rank):
    return spread(own_piece, "dp", owner_rank)


def dp_block(values, tensor_dim):
    slice_rows = values.shape[tensor_dim] // lax.axis_size("dp")
    return lax.dynamic_slice_in_dim(
        values, lax.axis_index("dp") * slice_rows, slice_rows, tensor_dim
    )


def tensor_block(values, tensor_dim):
    slice_rows = values.shape[tensor_dim] // lax.axis_size("tensor")
    return lax.dynamic_slice_in_dim(
        values, lax.axis_index("tensor") * slice_rows, slice_rows, tensor_dim
    )


def local(
    tokens,
    cotangent,
    region_ids,
    relative_index,
    shared_vectors,
    input_weight,
    head_bias,
    output_weight,
    expand_weight,
    expand_bias,
    reduce_weight,
    bias_table,
    moment_shared,
    moment_input,
    moment_head,
    moment_output,
    moment_expand,
    moment_bias,
    moment_reduce,
    moment_table,
):
    images, length, features = tokens.shape
    token_rows = images * length
    heads_here = bias_table.shape[1]
    head_size = head_bias.shape[1] // heads_here
    local_width = heads_here * head_size
    query_scale = head_size ** (-0.5)
    same_window, placement = position_tables()
    allowed = same_window & (region_ids[:, None] == region_ids[None, :])
    index_pick = index_table(relative_index, bias_table.shape[0])
    window_bias = jnp.dot(index_pick, bias_table, precision=highest).reshape(
        WIN * WIN, WIN * WIN, heads_here
    )
    bias_all = jnp.einsum("pi,ijh,qj->hpq", placement, window_bias, placement, precision=highest)
    input_low = input_weight.astype(jnp.bfloat16)
    output_low = output_weight.astype(jnp.bfloat16)
    expand_low = expand_weight.astype(jnp.bfloat16)
    reduce_low = reduce_weight.astype(jnp.bfloat16)
    inputs = tokens.astype(jnp.float32)
    normed, norm1_pull = jax.vjp(layer_norm, inputs, shared_vectors[0], shared_vectors[1])
    shifted = roll_tokens(normed, -SHIFT).astype(jnp.bfloat16).reshape(token_rows, features)
    projected = jnp.dot(shifted, input_low, preferred_element_type=jnp.float32)
    split_parts = projected.reshape(images, length, heads_here, 3, head_size)
    queries = (
        (split_parts[:, :, :, 0] + head_bias[0].reshape(heads_here, head_size)) * query_scale
    ).astype(jnp.bfloat16)
    key_rows = split_parts[:, :, :, 1].astype(jnp.bfloat16)
    value_rows = (split_parts[:, :, :, 2] + head_bias[1].reshape(heads_here, head_size)).astype(
        jnp.bfloat16
    )
    logits = attention_logits(queries, key_rows, bias_all, allowed)
    row_peak = jnp.max(logits, axis=-1, keepdims=True)
    log_total = row_peak + jnp.log(jnp.sum(jnp.exp(logits - row_peak), axis=-1, keepdims=True))
    attn_weights = jnp.exp(logits - log_total)
    context = jnp.einsum(
        "ghpq,gqhe->gphe",
        attn_weights.astype(jnp.bfloat16),
        value_rows,
        preferred_element_type=jnp.float32,
    )
    context_low = context.astype(jnp.bfloat16).reshape(token_rows, local_width)
    attended = (
        lax.psum(jnp.dot(context_low, output_low, preferred_element_type=jnp.float32), "tensor")
        + shared_vectors[2]
    )
    middle = inputs + roll_tokens(attended.reshape(images, length, features), SHIFT)
    normed2, norm2_pull = jax.vjp(layer_norm, middle, shared_vectors[3], shared_vectors[4])
    normed2_low = normed2.astype(jnp.bfloat16).reshape(token_rows, features)
    hidden = jnp.dot(normed2_low, expand_low, preferred_element_type=jnp.float32) + expand_bias
    activated, gelu_pull = jax.vjp(gelu_exact, hidden)
    activated_low = activated.astype(jnp.bfloat16)
    mixed_out = (
        lax.psum(jnp.dot(activated_low, reduce_low, preferred_element_type=jnp.float32), "tensor")
        + shared_vectors[5]
    )
    block_out = (middle + mixed_out.reshape(images, length, features)).astype(jnp.bfloat16)
    upstream = cotangent.reshape(token_rows, features)
    grad_reduce_bias = jnp.sum(upstream, axis=0, dtype=jnp.float32)
    grad_reduce = jnp.einsum(
        "rf,rd->fd", activated_low, upstream, preferred_element_type=jnp.float32
    )
    grad_activated = jnp.einsum(
        "rd,fd->rf", upstream, reduce_low, preferred_element_type=jnp.float32
    )
    grad_hidden = gelu_pull(grad_activated)[0]
    grad_expand_bias = jnp.sum(grad_hidden, axis=0)
    hidden_low = grad_hidden.astype(jnp.bfloat16)
    grad_expand = jnp.einsum(
        "rd,rf->df", normed2_low, hidden_low, preferred_element_type=jnp.float32
    )
    grad_normed2 = lax.psum(
        jnp.einsum("rf,df->rd", hidden_low, expand_low, preferred_element_type=jnp.float32),
        "tensor",
    )
    grad_middle, grad_gain2, grad_offset2 = norm2_pull(
        grad_normed2.reshape(images, length, features)
    )
    grad_middle = grad_middle + cotangent.astype(jnp.float32)
    grad_attended = roll_tokens(grad_middle, -SHIFT).reshape(token_rows, features)
    grad_output_bias = jnp.sum(grad_attended, axis=0)
    attended_low = grad_attended.astype(jnp.bfloat16)
    grad_output = jnp.einsum(
        "rc,rd->cd", context_low, attended_low, preferred_element_type=jnp.float32
    )
    grad_context = jnp.einsum(
        "rd,cd->rc", attended_low, output_low, preferred_element_type=jnp.float32
    )
    grad_context = grad_context.astype(jnp.bfloat16).reshape(images, length, heads_here, head_size)
    logits = attention_logits(queries, key_rows, bias_all, allowed)
    attn_weights = jnp.exp(logits - log_total)
    grad_weights = jnp.einsum(
        "gphe,gqhe->ghpq", grad_context, value_rows, preferred_element_type=jnp.float32
    )
    grad_logits = attn_weights * (
        grad_weights - jnp.sum(attn_weights * grad_weights, axis=-1, keepdims=True)
    )
    pair_grad = jnp.sum(grad_logits, axis=0)
    window_grad = jnp.einsum("pi,hpq,qj->ijh", placement, pair_grad, placement, precision=highest)
    grad_table = jnp.einsum(
        "nk,nh->kh",
        index_pick,
        window_grad.reshape(WIN * WIN * WIN * WIN, heads_here),
        precision=highest,
    )
    logits_low = grad_logits.astype(jnp.bfloat16)
    grad_queries = (
        jnp.einsum("ghpq,gqhe->gphe", logits_low, key_rows, preferred_element_type=jnp.float32)
        * query_scale
    )
    grad_keys = jnp.einsum(
        "ghpq,gphe->gqhe", logits_low, queries, preferred_element_type=jnp.float32
    )
    grad_values = jnp.einsum(
        "ghpq,gphe->gqhe",
        attn_weights.astype(jnp.bfloat16),
        grad_context,
        preferred_element_type=jnp.float32,
    )
    grad_head = jnp.stack(
        [
            jnp.sum(grad_queries, axis=(0, 1)).reshape(-1),
            jnp.sum(grad_values, axis=(0, 1)).reshape(-1),
        ]
    )
    grad_projected = jnp.stack([grad_queries, grad_keys, grad_values], axis=3).astype(jnp.bfloat16)
    grad_projected = grad_projected.reshape(token_rows, 3 * local_width)
    grad_input = jnp.einsum(
        "rd,rc->dc", shifted, grad_projected, preferred_element_type=jnp.float32
    )
    grad_shifted = lax.psum(
        jnp.einsum("rc,dc->rd", grad_projected, input_low, preferred_element_type=jnp.float32),
        "tensor",
    )
    grad_normed = roll_tokens(grad_shifted.reshape(images, length, features), SHIFT)
    grad_inputs, grad_gain1, grad_offset1 = norm1_pull(grad_normed)
    input_grad = grad_middle + grad_inputs
    grad_shared = jnp.stack(
        [grad_gain1, grad_offset1, grad_output_bias, grad_gain2, grad_offset2, grad_reduce_bias]
    )
    grad_scale = (token_rows * lax.axis_size("dp")) ** (-0.5)
    tensor_dims = (1, 0, 1, 0)
    matrix_factors = []
    for local_weight, tensor_dim in zip(
        (input_weight, output_weight, expand_weight, reduce_weight), tensor_dims
    ):
        whole_rows = local_weight.shape[0] * (lax.axis_size("tensor") if tensor_dim == 0 else 1)
        whole_cols = local_weight.shape[1] * (lax.axis_size("tensor") if tensor_dim == 1 else 1)
        matrix_factors.append(math.sqrt(max(1.0, whole_rows / whole_cols)))
    totals = lax.psum(
        (
            grad_shared,
            grad_input,
            grad_head,
            grad_output,
            grad_expand,
            grad_expand_bias,
            grad_reduce,
            grad_table,
        ),
        "dp",
    )
    gradients = [summed * grad_scale for summed in totals]
    moments = [
        moment_shared,
        moment_input,
        moment_head,
        moment_output,
        moment_expand,
        moment_bias,
        moment_reduce,
        moment_table,
    ]
    states = [
        moment_decay * moment + (1.0 - moment_decay) * gradient
        for moment, gradient in zip(moments, gradients)
    ]
    received = []
    full_states = (
        lax.all_gather(states[1], "tensor", axis=1, tiled=True),
        lax.all_gather(states[3], "tensor", axis=0, tiled=True),
        lax.all_gather(states[4], "tensor", axis=1, tiled=True),
        lax.all_gather(states[6], "tensor", axis=0, tiled=True),
    )
    for matrix_id in range(4):
        owner_rank = matrix_id % lax.axis_size("dp")
        orthogonal = lax.cond(
            lax.axis_index("dp") == owner_rank,
            orthogonalize,
            jnp.zeros_like,
            full_states[matrix_id],
        )
        received.append(send_back(tensor_block(orthogonal, tensor_dims[matrix_id]), owner_rank))
    matrix_updates = []
    for matrix_id in range(4):
        matrix_updates.append(
            dp_block(
                -matrix_rate * matrix_factors[matrix_id] * received[matrix_id],
                1 - tensor_dims[matrix_id],
            )
        )
    grad_outs = [
        gradients[0],
        dp_block(gradients[1], 0),
        gradients[2],
        dp_block(gradients[3], 1),
        dp_block(gradients[4], 0),
        gradients[5],
        dp_block(gradients[6], 1),
        gradients[7],
    ]
    state_outs = [
        states[0],
        dp_block(states[1], 0),
        states[2],
        dp_block(states[3], 1),
        dp_block(states[4], 0),
        states[5],
        dp_block(states[6], 1),
        states[7],
    ]
    return (
        block_out,
        input_grad,
        grad_outs[0],
        grad_outs[1],
        grad_outs[2],
        grad_outs[3],
        grad_outs[4],
        grad_outs[5],
        grad_outs[6],
        grad_outs[7],
        -vector_rate * state_outs[0],
        matrix_updates[0],
        -vector_rate * state_outs[2],
        matrix_updates[1],
        matrix_updates[2],
        -vector_rate * state_outs[5],
        matrix_updates[3],
        -vector_rate * state_outs[7],
        state_outs[0],
        state_outs[1],
        state_outs[2],
        state_outs[3],
        state_outs[4],
        state_outs[5],
        state_outs[6],
        state_outs[7],
    )


def solution(mesh):
    return jax.shard_map(
        local,
        mesh=mesh,
        in_specs=(
            P("dp", None, None),
            P("dp", None, None),
            P(),
            P(),
            P(),
            P(None, "tensor"),
            P(None, "tensor"),
            P("tensor", None),
            P(None, "tensor"),
            P("tensor"),
            P("tensor", None),
            P(None, "tensor"),
            P(),
            P(None, "tensor"),
            P(None, "tensor"),
            P("tensor", None),
            P(None, "tensor"),
            P("tensor"),
            P("tensor", None),
            P(None, "tensor"),
        ),
        out_specs=(
            P("dp", None, None),
            P("dp", None, None),
            P(),
            P("dp", "tensor"),
            P(None, "tensor"),
            P("tensor", "dp"),
            P("dp", "tensor"),
            P("tensor"),
            P("tensor", "dp"),
            P(None, "tensor"),
            P(),
            P("dp", "tensor"),
            P(None, "tensor"),
            P("tensor", "dp"),
            P("dp", "tensor"),
            P("tensor"),
            P("tensor", "dp"),
            P(None, "tensor"),
            P(),
            P("dp", "tensor"),
            P(None, "tensor"),
            P("tensor", "dp"),
            P("dp", "tensor"),
            P("tensor"),
            P("tensor", "dp"),
            P(None, "tensor"),
        ),
        check_vma=False,
    )
```

profile of v0, /device:TPU:0, one launch (start us, length us, event | category | flops | bytes accessed | tf_op | source)
XLA Modules:
  0.0 1091.5 jit_solution(15839427018356850085)
XLA Ops:
  66.0 94.3 %all-reduce.10.cloned.1.call-done = f32[2352,512]{1,0:T(8,128)} async-done(((f32[2352,512]{1,0:T(8,128)}), f32[2352,512]{1,0:T(8,128)}) %all-reduce.10.cloned.1.call-update) | async-done | bytes 4816912 | tf_op jit(solution)/shard_map/psum | solution.py:162
  165.5 6.2 reshape_reshape.7
  194.2 5.5 multiply_convert_fusion
  213.9 5.6 fusion.90
  222.0 82.7 %all-reduce.12.cloned.1.call-done = f32[2352,512]{1,0:T(8,128)} async-done(((f32[2352,512]{1,0:T(8,128)}), f32[2352,512]{1,0:T(8,128)}) %all-reduce.12.cloned.1.call-update) | async-done | bytes 4816912 | tf_op jit(solution)/shard_map/psum | solution.py:190
  304.7 5.6 reshape.373
  356.0 7.2 bitcast_reduce_fusion
  363.2 10.4 multiply_reduce_fusion.4
  373.6 7.5 fusion.142
  387.7 6.5 convert_element_type.142
  399.1 130.7 %all-reduce.16.cloned.1.call-done = (f32[512,384]{1,0:T(8,128)}, f32[128,512]{1,0:T(8,128)}, f32[512,512]{1,0:T(8,128)}, f32[512,512]{1,0:T(8,128)}) async-done(((f32[512,384]{1,0:T(8,128)}, f32[128,512]{1,0:T(8,128)}, f32[512,512]{1,0:T(8,128)}, f32[512,512]{1,0:T(8,128)}), (f32[512,384]{1,0:T(8,128)}, f32[128,512]{1,0:T(8,128)}, f32[512,512]{1,0:T(8,128)}, ...) | async-done | bytes 3145744 | tf_op jit(solution)/shard_map/psum | solution.py:268
  531.6 5.7 fusion.105
  540.9 6.2 reshape_reshape.8
  576.6 5.7 conditional.5
  584.0 150.9 %all-reduce.18.cloned.1.call-done = (f32[2352,512]{1,0:T(8,128)}, f32[12,14,14,512]{3,2,1,0:T(8,128)}) async-done(((f32[2352,512]{1,0:T(8,128)}, f32[12,14,14,512]{3,2,1,0:T(8,128)}), (f32[2352,512]{1,0:T(8,128)}, f32[12,14,14,512]{3,2,1,0:T(8,128)})) %all-reduce.18.cloned.1.call-update) | async-done | bytes 9633808 | tf_op jit(solution)/shard_map/psum | solution.py:172
  745.5 5.6 reshape.371
  768.0 74.4 %conditional.4 = (f32[512,1536]{1,0:T(8,128)}) conditional(s32[]{:T(128)} %convert_element_type.144, () %tuple.32, f32[512,1536]{1,0:T(8,128)} %all-gather.5.cloned.1.call-done), branch_computations={%region_35.36_spmd, %region_36.38_spmd} | conditional | flops 56387174400 | bytes 83886152 | solution.py:305
  772.5 9.1 fusion
  783.5 5.5 convolution_add_fusion.4
  796.4 5.5 convolution_add_fusion.3
  801.9 5.5 fusion.150
  809.3 5.5 convolution_add_fusion.2
  814.8 5.7 fusion.151
  822.4 5.5 convolution_add_fusion.1
  827.9 5.4 fusion.152
  835.2 7.0 convolution_add_fusion
  844.6 13.4 %conditional.6 = (f32[512,2048]{0,1:T(8,128)}) conditional(s32[]{:T(128)} %convert_element_type.146, () %tuple.34, f32[512,2048]{1,0:T(8,128)} %all-gather.9.cloned.1.call-done), branch_computations={%region_43.44_spmd, %region_44.46_spmd} | conditional | flops 72497233920 | bytes 113246280 | solution.py:305
  860.3 9.3 conditional.7
  876.9 111.8 %all-reduce = (f32[6,512]{1,0:T(8,128)S(1)}, f32[2,128]{1,0:T(2,128)S(1)}, f32[512]{0:T(512)S(1)}, f32[169,4]{0,1:T(4,128)S(1)}) all-reduce(f32[6,512]{1,0:T(8,128)S(1)} %stack.40, f32[2,128]{1,0:T(2,128)S(1)} %copy-done.51, f32[512]{0:T(512)S(1)} %copy-done.54, f32[169,4]{0,1:T(4,128)S(1)} %copy-done.52), channel_id=1, replica_groups=mesh['dp'=8,'tensor'=4] {'dp'}, use_global_device_ids=true, to_apply=%region_23.24 | all-reduce | flops 4516 | bytes 36128 | tf_op jit(solution)/shard_map/psum | solution.py:268
  991.1 6.4 add_convert_fusion
  997.5 6.4 add_add_fusion.2
  1003.9 74.5 %all-reduce.14.cloned.1.call-done = (f32[512,384]{1,0:T(8,128)}, f32[128,512]{0,1:T(8,128)}, f32[512,512]{0,1:T(8,128)}, f32[512,512]{0,1:T(8,128)}) async-done(((f32[512,384]{1,0:T(8,128)}, f32[128,512]{0,1:T(8,128)}, f32[512,512]{0,1:T(8,128)}, f32[512,512]{0,1:T(8,128)}), (f32[512,384]{1,0:T(8,128)}, f32[128,512]{0,1:T(8,128)}, f32[512,512]{0,1:T(8,128)}, ...) | async-done | bytes 3145744 | tf_op jit(solution)/shard_map/psum | solution.py:25
  (291 shorter events, 268.4 us)
Async XLA Ops:
  7.2 19.4 %copy-start = (f32[169,4]{0,1:T(4,128)S(1)}, f32[169,4]{0,1:T(4,128)}, u32[]{:S(2)}) copy-start(f32[169,4]{0,1:T(4,128)} %param.39) | copy-start | bytes 8116
  7.2 153.1 %all-reduce.10.cloned.1.call-start = ((), (), s32[]{:S(2)}) async-start(), calls=%async_computation | async-start | bytes 9633792 | tf_op jit(solution)/shard_map/psum | solution.py:162
  29.8 19.6 %copy-start.10 = (f32[4,196,196]{1,2,0:T(8,128)}, f32[4,196,196]{1,2,0:T(8,128)S(1)}, u32[]{:S(2)}) copy-start(f32[4,196,196]{1,2,0:T(8,128)S(1)} %fusion.122) | copy-start | bytes 1843972
  33.3 7.8 copy-start.49
  61.9 242.8 %all-reduce.12.cloned.1.call-start = ((), (), s32[]{:S(2)}) async-start(), calls=%async_computation.1 | async-start | bytes 9633792 | tf_op jit(solution)/shard_map/psum | solution.py:190
  208.8 321.0 %all-reduce.16.cloned.1.call-start = ((), (), s32[]{:S(2)}) async-start(), calls=%async_computation.7 | async-start | bytes 6291456 | tf_op jit(solution)/shard_map/psum | solution.py:268
  304.7 10.9 slice-start
  310.3 6.5 copy-start.5
  335.6 7.5 copy-start.18
  346.0 9.9 copy-start.11
  355.9 7.2 copy-start.24
  355.9 17.6 %slice-start.2 = ((s8[9830400]{0:T(1024)(128)(4,1)}), s8[4194304]{0:T(1024)(128)(4,1)S(1)}, s32[]{:S(2)}) async-start(s8[9830400]{0:T(1024)(128)(4,1)} %bitcast.240), calls=%async_computation.11 | async-start | bytes 8388608
  356.0 17.6 %slice-start.3 = ((s8[9830400]{0:T(1024)(128)(4,1)}), s8[4194304]{0:T(1024)(128)(4,1)S(1)}, s32[]{:S(2)}) async-start(s8[9830400]{0:T(1024)(128)(4,1)} %bitcast.240), calls=%async_computation.12 | async-start | bytes 8388608
  363.1 10.4 slice-start.4
  363.1 17.9 %slice-start.7 = ((s8[4718592]{0:T(1024)(128)(4,1)}), s8[4194304]{0:T(1024)(128)(4,1)S(1)}, s32[]{:S(2)}) async-start(s8[4718592]{0:T(1024)(128)(4,1)} %bitcast.244), calls=%async_computation.16 | async-start | bytes 8388608
  373.6 7.5 slice-start.8
  394.2 135.6 %copy-start.35 = (f32[128,512]{1,0:T(8,128)S(1)}, f32[128,512]{1,0:T(8,128)}, u32[]{:S(2)}) copy-start(f32[128,512]{1,0:T(8,128)} %param.43) | copy-start | bytes 786436
  399.0 177.6 %all-gather.7.cloned.1.call-start = ((), (), s32[]{:S(2)}) async-start(), calls=%async_computation.3 | async-start | bytes 1310720 | tf_op jit(solution)/shard_map/all_gather | solution.py:299
  531.6 203.3 %all-reduce.18.cloned.1.call-start = ((), (), s32[]{:S(2)}) async-start(), calls=%async_computation.8 | async-start | bytes 20643840 | tf_op jit(solution)/shard_map/psum | solution.py:172
  547.2 220.9 %all-gather.5.cloned.1.call-start = ((), (), s32[]{:S(2)}) async-start(), calls=%async_computation.2 | async-start | bytes 3932160 | tf_op jit(solution)/shard_map/all_gather | solution.py:298
  550.5 294.1 %all-gather.9.cloned.1.call-start = ((), (), s32[]{:S(2)}) async-start(), calls=%async_computation.4 | async-start | bytes 5242880 | tf_op jit(solution)/shard_map/all_gather | solution.py:300
  553.4 306.9 %all-gather.11.cloned.1.call-start = ((), (), s32[]{:S(2)}) async-start(), calls=%async_computation.5 | async-start | bytes 5242880 | tf_op jit(solution)/shard_map/all_gather | solution.py:301
  556.3 522.1 %all-reduce.14.cloned.1.call-start = ((), (), s32[]{:S(2)}) async-start(), calls=%async_computation.6 | async-start | bytes 6291456 | tf_op jit(solution)/shard_map/psum | solution.py:25
  734.9 7.8 slice-start.11
  772.5 11.0 %copy-start.13 = (f32[512,1536]{1,0:T(8,128)S(1)}, f32[512,1536]{1,0:T(8,128)}, u32[]{:S(2)}) copy-start(f32[512,1536]{1,0:T(8,128)} %param.1) | copy-start | bytes 9437188 | tf_op jit(solution)/shard_map/cond
  872.1 116.6 %copy-start.55 = (f32[2,128]{1,0:T(2,128)S(1)}, f32[2,128]{1,0:T(2,128)}, u32[]{:S(2)}) copy-start(f32[2,128]{1,0:T(2,128)} %param.42) | copy-start | bytes 3076
  872.1 117.2 %copy-start.53 = (f32[512]{0:T(512)S(1)}, f32[512]{0:T(512)}, u32[]{:S(2)}) copy-start(f32[512]{0:T(512)} %param.45) | copy-start | bytes 6148
  872.1 117.8 %copy-start.50 = (f32[169,4]{0,1:T(4,128)S(1)}, f32[169,4]{0,1:T(4,128)}, u32[]{:S(2)}) copy-start(f32[169,4]{0,1:T(4,128)} %param.47) | copy-start | bytes 8116
  872.2 118.4 %copy-start.41 = (f32[6,512]{1,0:T(8,128)S(1)}, f32[6,512]{1,0:T(8,128)}, u32[]{:S(2)}) copy-start(f32[6,512]{1,0:T(8,128)} %param.40) | copy-start | bytes 36868
  872.2 125.3 %slice-start.5 = ((s8[4915200]{0:T(1024)(128)(4,1)}), s8[720896]{0:T(1024)(128)(4,1)S(1)}, s32[]{:S(2)}) async-start(s8[4915200]{0:T(1024)(128)(4,1)} %bitcast.242), calls=%async_computation.14 | async-start | bytes 1441792
  991.1 6.4 slice-start.6
  997.5 87.2 %copy-start.1 = (f32[169,4]{0,1:T(4,128)S(1)}, f32[169,4]{0,1:T(4,128)}, u32[]{:S(2)}) copy-start(f32[169,4]{0,1:T(4,128)} %param.39) | copy-start | bytes 8116
  (44 other events, 173.6 us)
Sparse Core Ops, SparseCore 0:
  62.0 98.3 all-reduce.9
  208.9 95.7 all-reduce.11
  399.1 130.6 all-reduce.15
  531.7 15.6 all-gather.6
  550.0 184.8 all-reduce.17
  736.3 28.5 all-gather.4
  766.4 34.4 all-gather.8
  802.5 34.4 all-gather.10
  872.1 206.2 all-reduce.13
where the time goes:
time: 1100 us; the launch traced here: 1090 us
  waiting for transfers between devices  533 us (48%)
  matrix products  149 us (14%)
  local copies, waits for them, and re-layouts  135 us (12%)
  other arithmetic  124 us (11%)
  blocking collectives  112 us (10%)
  loops' own time  23.8 us (2%)
  between operations  15 us (1%)
    psum x1, waiting for transfers between devices, local(): lax.psum(jnp.dot(activated_low, reduce_low, preferred_element_type=jnp.fl...  151 us
    psum x1, waiting for transfers between devices, local(): lax.psum((grad_shared, grad_input, grad_head, grad_output, grad_expand, g...  131 us
    psum x1, blocking collectives, local(): lax.psum((grad_shared, grad_input, grad_head, grad_output, grad_expand, g...  112 us
    psum x1, waiting for transfers between devices, local(): lax.psum(jnp.dot(context_low, output_low, preferred_element_type=jnp.floa...  94.3 us
    psum x1, waiting for transfers between devices, local(): lax.psum(jnp.einsum('rf,df->rd', hidden_low, expand_low, preferred_elemen...  82.7 us
    psum x1, waiting for transfers between devices, spread(): return lax.psum(block, axis)  74.5 us
    dot_general x5, matrix products, orthogonalize(): gram_matrix = jnp.dot(iterate, iterate.T, precision=highest)  31 us
    dot_general x5, matrix products, orthogonalize(): jnp.dot(polynomial, iterate, precision=highest)  29.1 us
  transfers between devices with their start and end apart: 9, of which 5 were waited for; matrix products, arithmetic and copies ran while one was open for 18% of the time, Pallas kernels for 0%

commit v1 on v0

v1 whole, which is shorter than its diff:
```python
import functools
import math

import jax
import jax.numpy as jnp
import numpy as np
from jax import lax
from jax.experimental import pallas as pl
from jax.experimental.pallas import tpu as pltpu
from jax.sharding import PartitionSpec as P

SIDE = 14
WIN = 7
SHIFT = 3
NS_STEPS = 5
WIN2 = WIN * WIN
LEN = SIDE * SIDE
ROWS = 208
WPAD = 64
WROWS = 4 * WPAD

highest = lax.Precision.HIGHEST
norm_epsilon = 1e-05
moment_decay = 0.8
matrix_rate = 1.0
vector_rate = 1.0
quintic_coef = (3.4445, -4.775, 2.0315)
masked_logit = -1e30
f32 = jnp.float32
bf16 = jnp.bfloat16
VMEM = pl.BlockSpec(memory_space=pltpu.VMEM)


def params(limit_mib=56, **kw):
    return pltpu.CompilerParams(vmem_limit_bytes=limit_mib * 1024 * 1024, **kw)


def nn(a, b, **kw):
    return lax.dot_general(a, b, (((1,), (0,)), ((), ())), preferred_element_type=f32, **kw)


def nt(a, b, **kw):
    return lax.dot_general(a, b, (((1,), (1,)), ((), ())), preferred_element_type=f32, **kw)


def tn(a, b, **kw):
    return lax.dot_general(a, b, (((0,), (0,)), ((), ())), preferred_element_type=f32, **kw)


def window_tables():
    pick = np.zeros((WROWS, LEN), np.float32)
    place = np.zeros((4, WIN2), np.int32)
    for r in range(SIDE):
        for c in range(SIDE):
            w = (r // WIN) * 2 + c // WIN
            i = (r % WIN) * WIN + c % WIN
            source = ((r + SHIFT) % SIDE) * SIDE + (c + SHIFT) % SIDE
            pick[w * WPAD + i, source] = 1.0
            place[w, i] = r * SIDE + c
    return pick, place


def column_order(heads, size):
    width = 3 * heads * size
    order = np.zeros((width, width), np.float32)
    for h in range(heads):
        for part in range(3):
            for e in range(size):
                order[(h * 3 + part) * size + e, part * heads * size + h * size + e] = 1.0
    return order


def norm_parts(x):
    centred = x - jnp.mean(x, axis=-1, keepdims=True)
    scale = lax.rsqrt(jnp.mean(centred * centred, axis=-1, keepdims=True) + norm_epsilon)
    return centred * scale, scale


def norm_back(n, scale, gain, u):
    w = u * gain
    return scale * (
        w - jnp.mean(w, axis=-1, keepdims=True) - n * jnp.mean(w * n, axis=-1, keepdims=True)
    )


def head_blocks(x, masks):
    return jnp.concatenate([x * m for m in masks], axis=0)


def head_diag(r, masks):
    rows = r.shape[0] // 4
    out = r[0:rows] * masks[0]
    for h in range(1, 4):
        out = out + r[h * rows : (h + 1) * rows] * masks[h]
    return out


def head_masks(dtype):
    lane = lax.broadcasted_iota(jnp.int32, (1, 128), 1) // 32
    return [jnp.where(lane == h, 1.0, 0.0).astype(dtype) for h in range(4)]


def attn_forward(scale, t_ref, tok, w0, w1, w2, w3, hb, sv, bias, mask, pick, order, p_out, qkv_out,
                 sht_out, ctx_out, wcol):
    @pl.when(pl.program_id(0) == 0)
    def _():
        for k, w in enumerate((w0, w1, w2, w3)):
            wcol[k] = nn(w[...].astype(bf16), order[...]).astype(bf16)

    n, _ = norm_parts(tok[0].astype(f32))
    normed = (n * sv[0:1] + sv[1:2]).astype(bf16)
    shifted_f = nn(pick[...], normed)
    shifted = shifted_f.astype(bf16)
    sht_out[0] = shifted_f.T.astype(bf16)
    low_masks = head_masks(bf16)
    masks = head_masks(f32)
    for k in range(4):
        proj = nn(shifted, wcol[k])
        q = ((proj[:, 0:128] + hb[k, 0:1]) * scale).astype(bf16)
        kk = proj[:, 128:256].astype(bf16)
        v = (proj[:, 256:384] + hb[k, 1:2]).astype(bf16)
        qkv_out[0, k, :, 0:128] = q
        qkv_out[0, k, :, 128:256] = kk
        qkv_out[0, k, :, 256:384] = v
        windows = []
        for w in range(4):
            rows = slice(w * WPAD, (w + 1) * WPAD)
            logits = nt(kk[rows], head_blocks(q[rows], low_masks)) + (bias[k] + mask[w])
            e = jnp.exp(logits - jnp.max(logits, axis=0, keepdims=True))
            p = e * (1.0 / jnp.sum(e, axis=0, keepdims=True))
            p_out[0, k, w] = p
            windows.append(head_diag(tn(p.astype(bf16), v[rows]), masks).astype(bf16))
        ctx = jnp.concatenate(windows, axis=0)
        ctx_out[0, 0:LEN, k * 128 : (k + 1) * 128] = tn(pick[...], ctx).astype(bf16)
        ctx_out[0, LEN:ROWS, k * 128 : (k + 1) * 128] = jnp.zeros((ROWS - LEN, 128), bf16)


def feed_forward(images, t_ref, ctx, tok, cot, o0, o1, o2, o3, e0, e1, e2, e3, r0, r1, r2, r3, eb, sv,
                 out_ref, gmid_ref, gctx_ref, grad_ref, geb_ref, small_ref,
                 we, wr, wo, x_s, cot_s, mid_s, n2_s, n2t_s, cott_s, mix_s, gn2_s):
    rows = x_s.shape[0]
    x_s[...] = jnp.zeros_like(x_s)
    for i in range(images):
        x_s[i * ROWS : i * ROWS + LEN] = tok[i].astype(f32)
    for k, (o, e, r) in enumerate(((o0, e0, r0), (o1, e1, r1), (o2, e2, r2), (o3, e3, r3))):
        wo[k * 128 : (k + 1) * 128] = o[...].astype(bf16)
        for half in range(2):
            we[2 * k + half] = e[:, half * 256 : (half + 1) * 256].astype(bf16)
            wr[2 * k + half] = r[half * 256 : (half + 1) * 256].astype(bf16)
    attended = jnp.concatenate(
        [ctx[...].reshape(images * ROWS, 512), jnp.zeros((rows - images * ROWS, 512), bf16)], axis=0
    )
    mid_s[...] = x_s[...] + nn(attended, wo[...]) + sv[2:3]
    n2, _ = norm_parts(mid_s[...])
    n2f = n2 * sv[3:4] + sv[4:5]
    n2_s[...] = n2f.astype(bf16)
    n2t_s[...] = n2f.T.astype(bf16)
    x_s[...] = jnp.zeros_like(x_s)
    for i in range(images):
        x_s[i * ROWS : i * ROWS + LEN] = cot[i].astype(f32)
    cot_s[...] = x_s[...].astype(bf16)
    cott_s[...] = x_s[...].T.astype(bf16)
    mix_s[...] = jnp.zeros_like(mix_s)
    gn2_s[...] = jnp.zeros_like(gn2_s)

    def body(j, carry):
        hidden = nn(n2_s[...], we[j]) + eb[j]
        cdf = 0.5 * (1.0 + lax.erf(hidden * (1.0 / math.sqrt(2.0))))
        act = (hidden * cdf).astype(bf16)
        slope = cdf + hidden * jnp.exp(-0.5 * hidden * hidden) * (1.0 / math.sqrt(2.0 * math.pi))
        mix_s[...] += nn(act, wr[j])
        g_hidden = nt(cot_s[...], wr[j]) * slope
        geb_ref[j] = jnp.sum(g_hidden, axis=0, keepdims=True)
        low = g_hidden.astype(bf16)
        gn2_s[...] += nt(low, we[j])
        at = pl.multiple_of(lax.rem(j, 2) * 256, 256)
        grad_ref[j // 2, :, pl.ds(128 + at, 256)] = nn(n2t_s[...], low)
        grad_ref[j // 2, :, pl.ds(640 + at, 256)] = nn(cott_s[...], act)
        return carry

    lax.fori_loop(0, 8, body, 0)
    result = mid_s[...] + mix_s[...] + sv[5:6]
    for i in range(images):
        out_ref[i] = result[i * ROWS : i * ROWS + LEN].astype(bf16).astype(f32)
    n2, scale2 = norm_parts(mid_s[...])
    u = gn2_s[...]
    gmid = x_s[...] + norm_back(n2, scale2, sv[3:4], u)
    gmid_ref[...] = gmid
    small_ref[0:1] = jnp.sum(gmid, axis=0, keepdims=True)
    small_ref[1:2] = jnp.sum(u * n2, axis=0, keepdims=True)
    small_ref[2:3] = jnp.sum(u, axis=0, keepdims=True)
    small_ref[3:4] = jnp.sum(x_s[...], axis=0, keepdims=True)
    small_ref[4:8] = jnp.zeros((4, 512), f32)
    att_low = gmid.astype(bf16)
    gctx_ref[...] = nt(att_low, wo[...]).astype(bf16)[0 : images * ROWS].reshape(images, ROWS, 512)
    att_t = gmid.T.astype(bf16)
    g_out = nn(att_t, attended)
    for k in range(4):
        grad_ref[k, :, 0:128] = g_out[:, k * 128 : (k + 1) * 128]


def attn_backward(scale, p_in, qkv, gctx, sht, pick, order, gi_ref, plow_ref, gbias_ref, ghead_ref):
    @pl.when(pl.program_id(0) == 0)
    def _():
        gi_ref[...] = jnp.zeros_like(gi_ref)
        gbias_ref[...] = jnp.zeros_like(gbias_ref)
        ghead_ref[...] = jnp.zeros_like(ghead_ref)

    gwin = nn(pick[...], gctx[0, 0:LEN]).astype(bf16)
    low_masks = head_masks(bf16)
    masks = head_masks(f32)
    for k in range(4):
        q = qkv[0, k, :, 0:128]
        kk = qkv[0, k, :, 128:256]
        v = qkv[0, k, :, 256:384]
        parts = []
        bias_sum = None
        q_sum = None
        v_sum = None
        for w in range(4):
            rows = slice(w * WPAD, (w + 1) * WPAD)
            gbd = head_blocks(gwin[rows, k * 128 : (k + 1) * 128], low_masks)
            p = p_in[0, k, w]
            gp = nt(v[rows], gbd)
            gl = p * (gp - jnp.sum(p * gp, axis=0, keepdims=True))
            low = gl.astype(bf16)
            gq = head_diag(tn(low, kk[rows]), masks) * scale
            gk = nn(low, head_blocks(q[rows], low_masks))
            gv = nn(p.astype(bf16), gbd)
            bias_sum = gl if w == 0 else bias_sum + gl
            sq = jnp.sum(gq, axis=0, keepdims=True)
            sv_ = jnp.sum(gv, axis=0, keepdims=True)
            q_sum = sq if w == 0 else q_sum + sq
            v_sum = sv_ if w == 0 else v_sum + sv_
            parts.append(jnp.concatenate([gq, gk, gv], axis=1).astype(bf16))
        gbias_ref[k] += bias_sum
        ghead_ref[k, 0:1] += q_sum
        ghead_ref[k, 1:2] += v_sum
        plow = nt(jnp.concatenate(parts, axis=0), order[...]).astype(bf16)
        gi_ref[k] += nn(sht[0], plow)
        plow_ref[0, k, 0:LEN] = tn(pick[...], plow).astype(bf16)
        plow_ref[0, k, LEN:ROWS] = jnp.zeros((ROWS - LEN, plow.shape[1]), bf16)


def input_backward(t_ref, tok, gmid, plow, w0, w1, w2, w3, sv, out_ref, small_ref, wlow):
    @pl.when(pl.program_id(0) == 0)
    def _():
        small_ref[...] = jnp.zeros_like(small_ref)
        for k, w in enumerate((w0, w1, w2, w3)):
            wlow[k] = w[...].astype(bf16)

    u = nt(plow[0, 0], wlow[0])
    for k in range(1, 4):
        u = u + nt(plow[0, k], wlow[k])
    u = u[0:LEN]
    n, scale = norm_parts(tok[0].astype(f32))
    small_ref[0:1] += jnp.sum(u * n, axis=0, keepdims=True)
    small_ref[1:2] += jnp.sum(u, axis=0, keepdims=True)
    out_ref[0] = gmid[0:LEN] + norm_back(n, scale, sv[0:1], u)


def assemble(t_ref, a0, a1, a2, a3, out):
    for k, a in enumerate((a0, a1, a2, a3)):
        @pl.when(pl.program_id(0) == k)
        def _(a=a):
            out[...] = a[...].astype(out.dtype)


def gram_kernel(cuts, m_ref, g_ref):
    for m, (start, stop) in enumerate(cuts):
        part = m_ref[:, start:stop]
        g_ref[m] = nt(part, part, precision=highest)


def newton_schulz(g_ref, q_ref, a_s, b_s):
    g = g_ref[...]
    size = g.shape[0]
    row = lax.broadcasted_iota(jnp.int32, (size, size), 0)
    col = lax.broadcasted_iota(jnp.int32, (size, size), 1)
    eye = jnp.where(row == col, 1.0, 0.0)
    inv = 1.0 / (jnp.sum(g * eye) + 1e-07)
    a_s[...] = g * inv
    c0, c1, c2 = quintic_coef
    for step in range(NS_STEPS):
        a = a_s[...]
        b_s[...] = c0 * eye + c1 * a + c2 * nn(a, a, precision=highest)
        if step == 0:
            q_ref[...] = b_s[...]
        else:
            q_ref[...] = nn(b_s[...], q_ref[...], precision=highest)
        if step < NS_STEPS - 1:
            a_s[...] = nn(b_s[...], nn(b_s[...], a_s[...], precision=highest), precision=highest)
    q_ref[...] = q_ref[...] * lax.rsqrt(jnp.full((1, 1), 1.0, f32) / inv)


def final_kernel(cuts, factors, q_ref, m_ref, u_ref):
    for m, (start, stop) in enumerate(cuts):
        u_ref[:, start:stop] = (-matrix_rate * factors[m]) * nn(
            q_ref[m], m_ref[:, start:stop], precision=highest
        )


def xor_tensor(x, k):
    return lax.ppermute(x, "tensor", [(i, i ^ k) for i in range(lax.axis_size("tensor"))])


def xor_dp(x, k):
    return lax.ppermute(x, "dp", [(i, i ^ k) for i in range(lax.axis_size("dp"))])


def gather_tensor(block):
    near = xor_tensor(block, 1)
    far = xor_tensor(block, 2)
    return [block, near, far, xor_tensor(far, 1)]


def scatter_tensor(blocks):
    got = xor_tensor(jnp.stack([blocks[1], blocks[3]]), 1)
    own = blocks[0] + got[0]
    far = blocks[2] + got[1]
    return own + xor_tensor(far, 2)


def scatter_dp(values):
    count = lax.axis_size("dp")
    piece = values.shape[0] // count
    me = lax.axis_index("dp")
    cut = values.reshape(count, piece, values.shape[1])
    bit = 1
    while bit < count:
        here = (me // bit) % 2
        cut = cut.reshape(cut.shape[0] // 2, 2, piece, values.shape[1])
        keep = lax.dynamic_index_in_dim(cut, here, 1, keepdims=False)
        send = lax.dynamic_index_in_dim(cut, 1 - here, 1, keepdims=False)
        cut = keep + xor_dp(send, bit)
        bit *= 2
    return cut.reshape(piece, values.shape[1])


def gather_dp(piece):
    count = lax.axis_size("dp")
    me = lax.axis_index("dp")
    rows, cols = piece.shape
    whole = piece.reshape(1, rows, cols)
    bit = count // 2
    while bit >= 1:
        here = (me // bit) % 2
        got = xor_dp(whole, bit)
        pair = jnp.where(here == 0, jnp.stack([whole, got], 1), jnp.stack([got, whole], 1))
        whole = pair.reshape(-1, rows, cols)
        bit //= 2
    return whole.reshape(count * rows, cols)


def join_images(t, parts, dtype):
    images, length, features = parts[0].shape

    def source(k):
        return lambda a, i, t_ref: (jnp.where(a == k, i, jnp.where(a < k, 0, images - 1)), 0, 0)

    return pl.pallas_call(
        assemble,
        grid_spec=pltpu.PrefetchScalarGridSpec(
            num_scalar_prefetch=1,
            grid=(4, images),
            in_specs=[pl.BlockSpec((1, length, features), source(k)) for k in range(4)],
            out_specs=pl.BlockSpec(
                (1, length, features), lambda a, i, t_ref: ((t_ref[0] ^ a) * images + i, 0, 0)
            ),
        ),
        out_shape=jax.ShapeDtypeStruct((4 * images, length, features), dtype),
        compiler_params=params(),
        name="join_images",
    )(t, *parts)


def local(
    tokens,
    cotangent,
    region_ids,
    relative_index,
    shared_vectors,
    input_weight,
    head_bias,
    output_weight,
    expand_weight,
    expand_bias,
    reduce_weight,
    bias_table,
    moment_shared,
    moment_input,
    moment_head,
    moment_output,
    moment_expand,
    moment_bias,
    moment_reduce,
    moment_table,
):
    nt_axis = lax.axis_size("tensor")
    me_t = lax.axis_index("tensor")
    me_d = lax.axis_index("dp")
    nd = lax.axis_size("dp")
    all_images, length, features = tokens.shape
    images = all_images // nt_axis
    heads = bias_table.shape[1]
    head_size = head_bias.shape[1] // heads
    width = heads * head_size
    hidden_here = expand_weight.shape[1]
    table_rows = bias_table.shape[0]
    query_scale = head_size ** (-0.5)
    t_arr = me_t.astype(jnp.int32).reshape(1)
    rows = -(-images * ROWS // 128) * 128

    small_in = jnp.concatenate(
        [
            bias_table.T.reshape(-1),
            head_bias.reshape(-1),
            expand_bias.reshape(-1),
            jnp.zeros((4 * 512 - table_rows * heads - 2 * width - hidden_here,), f32)
            if table_rows * heads + 2 * width + hidden_here < 2048
            else jnp.zeros((0,), f32),
        ]
    )
    smalls = gather_tensor(small_in)
    w_in = gather_tensor(input_weight)
    w_out = gather_tensor(output_weight)
    w_exp = gather_tensor(expand_weight)
    w_red = gather_tensor(reduce_weight)
    tables = jnp.concatenate([s[: table_rows * heads].reshape(heads, table_rows) for s in smalls])
    at = table_rows * heads
    hb = jnp.stack([s[at : at + 2 * width].reshape(2, width) for s in smalls])
    at += 2 * width
    eb = jnp.concatenate([s[at : at + hidden_here] for s in smalls]).reshape(8, 1, hidden_here // 2)

    pick_np, place_np = window_tables()
    pick = jnp.asarray(pick_np, bf16)
    order = jnp.asarray(column_order(heads, head_size), bf16)
    rel_t = jnp.pad(relative_index.T, ((0, 0), (0, WPAD - WIN2)), constant_values=-1)
    pick_table = (jnp.arange(table_rows)[:, None] == rel_t.reshape(1, -1)).astype(f32)
    bias = jnp.dot(tables, pick_table, precision=highest).reshape(4, heads, WIN2, WPAD)
    bias = jnp.pad(bias.transpose(0, 2, 1, 3), ((0, 0), (0, WPAD - WIN2), (0, 0), (0, 0)))
    bias = bias.reshape(4, WPAD, heads * WPAD)
    region = region_ids[place_np]
    allowed = jnp.pad(
        region[:, :, None] == region[:, None, :],
        ((0, 0), (0, 0), (0, WPAD - WIN2)),
        constant_values=True,
    )
    allowed = jnp.pad(allowed, ((0, 0), (0, WPAD - WIN2), (0, 0)))
    mask = jnp.tile(jnp.where(allowed, 0.0, masked_logit).astype(f32), (1, 1, heads))

    whole = lambda *shape: pl.BlockSpec(shape, lambda i, *_: (0,) * len(shape))
    one = lambda *shape: pl.BlockSpec((1,) + shape, lambda i, *_: (i,) + (0,) * len(shape))
    tok_one = pl.BlockSpec((1, length, features), lambda i, t: (t[0] * images + i, 0, 0))

    probs, qkv, sht, ctx = pl.pallas_call(
        functools.partial(attn_forward, query_scale),
        grid_spec=pltpu.PrefetchScalarGridSpec(
            num_scalar_prefetch=1,
            grid=(images,),
            in_specs=[tok_one]
            + [whole(features, 3 * width)] * 4
            + [
                whole(4, 2, width),
                whole(6, features),
                whole(4, WPAD, heads * WPAD),
                whole(4, WPAD, heads * WPAD),
                whole(WROWS, LEN),
                whole(3 * width, 3 * width),
            ],
            out_specs=[
                one(4, 4, WPAD, heads * WPAD),
                one(4, WROWS, 3 * width),
                one(features, WROWS),
                one(ROWS, 4 * width),
            ],
            scratch_shapes=[pltpu.VMEM((4, features, 3 * width), bf16)],
        ),
        out_shape=[
            jax.ShapeDtypeStruct((images, 4, 4, WPAD, heads * WPAD), f32),
            jax.ShapeDtypeStruct((images, 4, WROWS, 3 * width), bf16),
            jax.ShapeDtypeStruct((images, features, WROWS), bf16),
            jax.ShapeDtypeStruct((images, ROWS, 4 * width), bf16),
        ],
        compiler_params=params(),
        name="attn_forward",
    )(t_arr, tokens, *w_in, hb, shared_vectors, bias, mask, pick, order)

    tok_all = pl.BlockSpec((images, length, features), lambda i, t: (t[0], 0, 0))
    wide = width + 2 * hidden_here
    block_part, gmid, gctx, grads_a, geb, small_a = pl.pallas_call(
        functools.partial(feed_forward, images),
        grid_spec=pltpu.PrefetchScalarGridSpec(
            num_scalar_prefetch=1,
            grid=(1,),
            in_specs=[whole(images, ROWS, 4 * width), tok_all, tok_all]
            + [whole(width, features)] * 4
            + [whole(features, hidden_here)] * 4
            + [whole(hidden_here, features)] * 4
            + [whole(8, 1, hidden_here // 2), whole(6, features)],
            out_specs=[
                whole(images, length, features),
                whole(rows, features),
                whole(images, ROWS, 4 * width),
                whole(4, features, wide),
                whole(8, 1, hidden_here // 2),
                whole(8, features),
            ],
            scratch_shapes=[
                pltpu.VMEM((8, features, hidden_here // 2), bf16),
                pltpu.VMEM((8, hidden_here // 2, features), bf16),
                pltpu.VMEM((4 * width, features), bf16),
                pltpu.VMEM((rows, features), f32),
                pltpu.VMEM((rows, features), bf16),
                pltpu.VMEM((rows, features), f32),
                pltpu.VMEM((rows, features), bf16),
                pltpu.VMEM((features, rows), bf16),
                pltpu.VMEM((features, rows), bf16),
                pltpu.VMEM((rows, features), f32),
                pltpu.VMEM((rows, features), f32),
            ],
        ),
        out_shape=[
            jax.ShapeDtypeStruct((images, length, features), f32),
            jax.ShapeDtypeStruct((rows, features), f32),
            jax.ShapeDtypeStruct((images, ROWS, 4 * width), bf16),
            jax.ShapeDtypeStruct((4, features, wide), f32),
            jax.ShapeDtypeStruct((8, 1, hidden_here // 2), f32),
            jax.ShapeDtypeStruct((8, features), f32),
        ],
        compiler_params=params(),
        name="feed_forward",
    )(t_arr, ctx, tokens, cotangent, *w_out, *w_exp, *w_red, eb, shared_vectors)

    grads_i, plow, gbias, ghead = pl.pallas_call(
        functools.partial(attn_backward, query_scale),
        grid=(images,),
        in_specs=[
            one(4, 4, WPAD, heads * WPAD),
            one(4, WROWS, 3 * width),
            one(ROWS, 4 * width),
            one(features, WROWS),
            whole(WROWS, LEN),
            whole(3 * width, 3 * width),
        ],
        out_specs=[
            whole(4, features, 3 * width),
            one(4, ROWS, 3 * width),
            whole(4, WPAD, heads * WPAD),
            whole(4, 2, width),
        ],
        out_shape=[
            jax.ShapeDtypeStruct((4, features, 3 * width), f32),
            jax.ShapeDtypeStruct((images, 4, ROWS, 3 * width), bf16),
            jax.ShapeDtypeStruct((4, WPAD, heads * WPAD), f32),
            jax.ShapeDtypeStruct((4, 2, width), f32),
        ],
        compiler_params=params(),
        name="attn_backward",
    )(probs, qkv, gctx, sht, pick, order)

    grad_part, small_i = pl.pallas_call(
        input_backward,
        grid_spec=pltpu.PrefetchScalarGridSpec(
            num_scalar_prefetch=1,
            grid=(images,),
            in_specs=[
                tok_one,
                pl.BlockSpec((ROWS, features), lambda i, t: (i, 0)),
                one(4, ROWS, 3 * width),
            ]
            + [whole(features, 3 * width)] * 4
            + [whole(6, features)],
            out_specs=[one(length, features), whole(8, features)],
            scratch_shapes=[pltpu.VMEM((4, features, 3 * width), bf16)],
        ),
        out_shape=[
            jax.ShapeDtypeStruct((images, length, features), f32),
            jax.ShapeDtypeStruct((8, features), f32),
        ],
        compiler_params=params(),
        name="input_backward",
    )(t_arr, tokens, gmid, plow, *w_in, shared_vectors)

    block_out = join_images(t_arr, gather_tensor(block_part), bf16)
    input_grad = join_images(t_arr, gather_tensor(grad_part), f32)

    gb = gbias[:, :WIN2].reshape(4, WIN2, heads, WPAD).transpose(0, 2, 1, 3)
    gtable = lax.dot_general(
        gb.reshape(4 * heads, -1), pick_table, (((1,), (1,)), ((), ())), precision=highest
    ).reshape(4, heads * table_rows)
    shared_rows = jnp.concatenate([small_i[0:2], small_a[0:4]])
    block_small = jnp.concatenate(
        [gtable, ghead.reshape(4, -1), geb.reshape(4, hidden_here)], axis=1
    )
    got = xor_tensor(
        jnp.concatenate([block_small[1], block_small[3], shared_rows.reshape(-1)]), 1
    )
    n_small = block_small.shape[1]
    own_small = block_small[0] + got[:n_small]
    far_small = block_small[2] + got[n_small : 2 * n_small]
    shared_sum = shared_rows.reshape(-1) + got[2 * n_small :]
    got = xor_tensor(jnp.concatenate([far_small, shared_sum]), 2)
    vector = jnp.concatenate([own_small, shared_sum]) + got
    vector = lax.psum(vector, "dp")

    grad_scale = (all_images * length * nd) ** (-0.5)
    at = heads * table_rows
    gradients = {
        "table": vector[:at].reshape(heads, table_rows).T,
        "head": vector[at : at + 2 * width].reshape(2, width),
        "bias": vector[at + 2 * width : n_small],
        "shared": vector[n_small:].reshape(6, features),
    }
    moments = dict(table=moment_table, head=moment_head, bias=moment_bias, shared=moment_shared)
    gradients = {k: v * grad_scale for k, v in gradients.items()}
    states = {
        k: moment_decay * moments[k] + (1.0 - moment_decay) * gradients[k] for k in gradients
    }

    own = scatter_tensor(
        [jnp.concatenate([grads_i[k], grads_a[k]], axis=1) for k in range(4)]
    )
    grad_piece = scatter_dp(own) * grad_scale
    piece = features // nd
    row_at = me_d * piece
    moment_piece = jnp.concatenate(
        [
            lax.dynamic_slice_in_dim(moment_input, row_at, piece, 0),
            lax.dynamic_slice_in_dim(moment_output, row_at, piece, 1).T,
            lax.dynamic_slice_in_dim(moment_expand, row_at, piece, 0),
            lax.dynamic_slice_in_dim(moment_reduce, row_at, piece, 1).T,
        ],
        axis=1,
    )
    state_piece = moment_decay * moment_piece + (1.0 - moment_decay) * grad_piece
    state = gather_dp(state_piece)
    ends = np.cumsum([0, 3 * width, width, hidden_here, hidden_here])
    cuts = [(int(a), int(b)) for a, b in zip(ends[:-1], ends[1:])]
    grams = pl.pallas_call(
        functools.partial(gram_kernel, cuts),
        in_specs=[VMEM],
        out_specs=VMEM,
        out_shape=jax.ShapeDtypeStruct((4, features, features), f32),
        compiler_params=params(),
        name="gram",
    )(state)
    gram = scatter_tensor(
        [lax.dynamic_index_in_dim(grams, me_t ^ k, 0, keepdims=False) for k in range(4)]
    )
    poly = pl.pallas_call(
        newton_schulz,
        in_specs=[VMEM],
        out_specs=VMEM,
        out_shape=jax.ShapeDtypeStruct((features, features), f32),
        scratch_shapes=[pltpu.VMEM((features, features), f32)] * 2,
        compiler_params=params(),
        name="newton_schulz",
    )(gram)
    poly_rows = jnp.stack(gather_tensor(lax.dynamic_slice_in_dim(poly, row_at, piece, 0)))
    poly_rows = jnp.stack(
        [lax.dynamic_index_in_dim(poly_rows, me_t ^ m, 0, keepdims=False) for m in range(4)]
    )
    shapes = [
        (features, 3 * width * nt_axis),
        (width * nt_axis, features),
        (features, hidden_here * nt_axis),
        (hidden_here * nt_axis, features),
    ]
    factors = [math.sqrt(max(1.0, a / b)) for a, b in shapes]
    update = pl.pallas_call(
        functools.partial(final_kernel, cuts, factors),
        in_specs=[VMEM, VMEM],
        out_specs=VMEM,
        out_shape=jax.ShapeDtypeStruct((piece, ends[-1]), f32),
        compiler_params=params(),
        name="update",
    )(poly_rows, state)

    def split(values):
        a, b, c, d = [values[:, s:e] for s, e in cuts]
        return a, b.T, c, d.T

    grad_m = split(grad_piece)
    state_m = split(state_piece)
    update_m = split(update)
    return (
        block_out,
        input_grad,
        gradients["shared"],
        grad_m[0],
        gradients["head"],
        grad_m[1],
        grad_m[2],
        gradients["bias"],
        grad_m[3],
        gradients["table"],
        -vector_rate * states["shared"],
        update_m[0],
        -vector_rate * states["head"],
        update_m[1],
        update_m[2],
        -vector_rate * states["bias"],
        update_m[3],
        -vector_rate * states["table"],
        states["shared"],
        state_m[0],
        states["head"],
        state_m[1],
        state_m[2],
        states["bias"],
        state_m[3],
        states["table"],
    )


def solution(mesh):
    return jax.shard_map(
        local,
        mesh=mesh,
        in_specs=(
            P("dp", None, None),
            P("dp", None, None),
            P(),
            P(),
            P(),
            P(None, "tensor"),
            P(None, "tensor"),
            P("tensor", None),
            P(None, "tensor"),
            P("tensor"),
            P("tensor", None),
            P(None, "tensor"),
            P(),
            P(None, "tensor"),
            P(None, "tensor"),
            P("tensor", None),
            P(None, "tensor"),
            P("tensor"),
            P("tensor", None),
            P(None, "tensor"),
        ),
        out_specs=(
            P("dp", None, None),
            P("dp", None, None),
            P(),
            P("dp", "tensor"),
            P(None, "tensor"),
            P("tensor", "dp"),
            P("dp", "tensor"),
            P("tensor"),
            P("tensor", "dp"),
            P(None, "tensor"),
            P(),
            P("dp", "tensor"),
            P(None, "tensor"),
            P("tensor", "dp"),
            P("dp", "tensor"),
            P("tensor"),
            P("tensor", "dp"),
            P(None, "tensor"),
            P(),
            P("dp", "tensor"),
            P(None, "tensor"),
            P("tensor", "dp"),
            P("dp", "tensor"),
            P("tensor"),
            P("tensor", "dp"),
            P(None, "tensor"),
        ),
        check_vma=False,
    )
```

time: 1100 us -> 611 us (0.56)
  waiting for transfers between devices: 533 us -> 331 us
  matrix products: 149 us -> 2.62 us
  Pallas kernels: 0 us -> 132 us
  other arithmetic: 124 us -> 27.2 us
  local copies, waits for them, and re-layouts: 135 us -> 49.2 us
  blocking collectives: 112 us -> 38.1 us
  starting transfers between devices: 0.37 us -> 24.4 us
  loops' own time: 23.8 us -> 0 us
  between operations: 15 us -> 1.58 us
    psum x5 -> x0, waiting for transfers between devices: 533 us -> none  [the longest x1 151 us: local(): lax.psum(jnp.dot(activated_low, reduce_low, preferred_element_type=jnp.fl...]
    ppermute x0 -> x36, waiting for transfers between devices: none -> 331 us  [the longest x30 201 us: xor_tensor(): lax.ppermute(x, 'tensor', [(i, i ^ k) for i in range(lax.axis_size('tenso...]
    dot_general x39 -> x2, matrix products: 149 us -> 2.62 us  [the longest x1 1.52 us: local(): jnp.dot(tables, pick_table, precision=highest).reshape(4, heads, WIN2, WPAD)]
    pallas_call x0 -> x9, Pallas kernels: none -> 132 us  [the longest x1 32.6 us: local(): pl.pallas_call(newton_schulz, in_specs=[VMEM], out_specs=VMEM, out_shape=...]
    psum x1, blocking collectives: 112 us -> 38.1 us  [local(): vector = lax.psum(vector, 'dp')]
    reduce_sum x19 -> x0, other arithmetic: 50.6 us -> none  [the longest x8 23.1 us: layer_norm(): return centred * lax.rsqrt(variance + norm_epsilon) * gain_vector + offset]
    reshape x12 -> x11, local copies, waits for them, and re-layouts: 46.8 us -> 5.43 us  [the longest x1 2.07 us: local(): bias = bias.reshape(4, WPAD, heads * WPAD)]
    convert_element_type x7 -> x0, local copies, waits for them, and re-layouts: 27.7 us -> none  [the longest x2 9.82 us: local(): jnp.stack([grad_queries, grad_keys, grad_values], axis=3)]
  transfers between devices with their start and end apart: 9 -> 36, of which waited for: 5 -> 15; matrix products, arithmetic and copies ran while one was open for 18% -> 6% of each run, Pallas kernels for 0% -> 7%
where the time goes in v1:
time: 611 us; the launch traced here: 606 us
  waiting for transfers between devices  331 us (54%)
  Pallas kernels  132 us (22%)
  local copies, waits for them, and re-layouts  49.2 us (8%)
  blocking collectives  38.1 us (6%)
  other arithmetic  27.2 us (4%)
  starting transfers between devices  24.4 us (4%)
    ppermute x30, waiting for transfers between devices, xor_tensor(): lax.ppermute(x, 'tensor', [(i, i ^ k) for i in range(lax.axis_size('tenso...  201 us
    ppermute x6, waiting for transfers between devices, xor_dp(): lax.ppermute(x, 'dp', [(i, i ^ k) for i in range(lax.axis_size('dp'))])  130 us
    psum x1, blocking collectives, local(): vector = lax.psum(vector, 'dp')  38.1 us
    pallas_call x1, Pallas kernels, local(): pl.pallas_call(newton_schulz, in_specs=[VMEM], out_specs=VMEM, out_shape=...  32.6 us
    pallas_call x1, Pallas kernels, local(): pl.pallas_call(functools.partial(feed_forward, images), grid_spec=pltpu.P...  24.6 us
    pallas_call x1, Pallas kernels, local(): pl.pallas_call(functools.partial(attn_backward, query_scale), grid=(image...  21.1 us
    ppermute x30, starting transfers between devices, xor_tensor(): lax.ppermute(x, 'tensor', [(i, i ^ k) for i in range(lax.axis_size('tenso...  17.8 us
    pallas_call x2, Pallas kernels, join_images(): pl.pallas_call(assemble, grid_spec=pltpu.PrefetchScalarGridSpec(num_scala...  17.8 us
  transfers between devices with their start and end apart: 36, of which 15 were waited for; matrix products, arithmetic and copies ran while one was open for 6% of the time, Pallas kernels for 7%

profile of v1, /device:TPU:0, one launch (start us, length us, event | category | flops | bytes accessed | tf_op | source)
XLA Modules:
  0.0 606.3 jit_solution(10354536273207087035)
XLA Ops:
  0.7 3.0 collective-permute-start.10
  7.4 59.2 %collective-permute-done.4 = f32[2048]{0:T(1024)S(1)} collective-permute-done((f32[2048]{0:T(1024)S(1)}, f32[2048]{0:T(1024)S(1)}, u32[]{:S(2)}, u32[]{:S(2)}) %collective-permute-start.4) | collective-permute-done | bytes 8224 | tf_op jit(solution)/shard_map/ppermute | solution.py:304
  74.4 3.2 collective-permute-done.7.o2
  79.3 2.1 tile.10.mask
  92.2 15.3 %attn_forward.1 = (f32[3,4,4,64,256]{4,3,2,1,0:T(8,128)}, bf16[3,4,256,384]{3,2,1,0:T(8,128)(2,1)}, bf16[3,512,256]{2,1,0:T(8,128)(2,1)}, bf16[3,208,512]{2,1,0:T(8,128)(2,1)}) custom-call(s32[1]{0:T(128)} %bitcast.t_ref, bf16[12,196,512]{2,1,0:T(8,128)(2,1)} %tok.5, f32[512,384]{1,0:T(8,128)} %w0.3, f32[512,384]{1,0:T(8,128)} %copy-done.4, ...), custom_call_target="tpu_custom_call" | custom-call | tf_op jit(solution)/shard_map/attn_forward/pallas_call | solution.py:456
  107.5 24.6 %feed_forward.1 = (f32[3,196,512]{2,1,0:T(8,128)}, f32[640,512]{1,0:T(8,128)}, bf16[3,208,512]{2,1,0:T(8,128)(2,1)}, f32[4,512,1152]{2,1,0:T(8,128)}, f32[8,1,256]{2,1,0:T(1,128)}, /*index=5*/f32[8,512]{1,0:T(8,128)}) custom-call(s32[1]{0:T(128)} %bitcast.t_ref, bf16[3,208,512]{2,1,0:T(8,128)(2,1)} %get-tuple-element.42.ctx, bf16[12,196,512]{2,1,0:T(8,128)(2,1)} %tok.5, ...), custom_call_target="tpu_custom_call" | custom-call | tf_op jit(solution)/shard_map/feed_forward/pallas_call | solution.py:491
  132.1 21.1 %attn_backward.1 = (f32[4,512,384]{2,1,0:T(8,128)}, bf16[3,4,208,384]{3,2,1,0:T(8,128)(2,1)}, f32[4,64,256]{2,1,0:T(8,128)}, f32[4,2,128]{2,1,0:T(2,128)}) custom-call(f32[3,4,4,64,256]{4,3,2,1,0:T(8,128)} %get-tuple-element.45.p_in, bf16[3,4,256,384]{3,2,1,0:T(8,128)(2,1)} %get-tuple-element.46.qkv, bf16[3,208,512]{2,1,0:T(8,128)(2,1)} %get-tuple-element.47.gctx, ...), custom_call_target="tpu_custom_call" | custom-call | tf_op jit(solution)/shard_map/attn_backward/pallas_call | solution.py:535
  153.3 2.9 slice_bitcast_fusion.9
  156.2 4.4 slice_bitcast_fusion.5
  162.1 10.0 %collective-permute-done.23 = f32[2,512,1536]{2,1,0:T(8,128)S(1)} collective-permute-done((f32[2,512,1536]{2,1,0:T(8,128)S(1)}, f32[2,512,1536]{2,1,0:T(8,128)S(1)}, u32[]{:S(2)}, u32[]{:S(2)}) %collective-permute-start.23) | collective-permute-done | bytes 6291488 | tf_op jit(solution)/shard_map/ppermute | solution.py:304
  172.1 2.4 fusion
  177.4 68.9 %collective-permute-done.24 = f32[512,1536]{1,0:T(8,128)} collective-permute-done((f32[512,1536]{1,0:T(8,128)}, f32[512,1536]{1,0:T(8,128)}, u32[]{:S(2)}, u32[]{:S(2)}) %collective-permute-start.24) | collective-permute-done | bytes 3145760 | tf_op jit(solution)/shard_map/ppermute | solution.py:304
  246.3 3.7 fusion.2
  253.5 34.2 %collective-permute-done.25 = f32[4,64,1536]{2,1,0:T(8,128)} collective-permute-done((f32[4,64,1536]{2,1,0:T(8,128)S(1)}, f32[4,64,1536]{2,1,0:T(8,128)}, u32[]{:S(2)}, u32[]{:S(2)}) %collective-permute-start.25) | collective-permute-done | bytes 1572896 | tf_op jit(solution)/shard_map/ppermute | solution.py:308
  294.2 13.8 %collective-permute-done.26 = f32[2,64,1536]{2,1,0:T(8,128)} collective-permute-done((f32[2,64,1536]{2,1,0:T(8,128)S(1)}, f32[2,64,1536]{2,1,0:T(8,128)}, u32[]{:S(2)}, u32[]{:S(2)}) %collective-permute-start.26) | collective-permute-done | bytes 786464 | tf_op jit(solution)/shard_map/ppermute | solution.py:308
  309.3 2.5 collective-permute-start.27
  314.9 12.4 %collective-permute-done.27 = f32[1,64,1536]{2,1,0:T(8,128)S(1)} collective-permute-done((f32[1,64,1536]{2,1,0:T(8,128)S(1)}, f32[1,64,1536]{2,1,0:T(8,128)S(1)}, u32[]{:S(2)}, u32[]{:S(2)}) %collective-permute-start.27) | collective-permute-done | bytes 393248 | tf_op jit(solution)/shard_map/ppermute | solution.py:308
  329.0 19.5 %collective-permute-done.28 = f32[1,64,1536]{2,1,0:T(8,128)S(1)} collective-permute-done((f32[1,64,1536]{2,1,0:T(8,128)S(1)}, f32[1,64,1536]{2,1,0:T(8,128)S(1)}, u32[]{:S(2)}, u32[]{:S(2)}) %collective-permute-start.28) | collective-permute-done | bytes 393248 | tf_op jit(solution)/shard_map/ppermute | solution.py:308
  348.7 17.8 %collective-permute-done.29 = f32[2,64,1536]{2,1,0:T(8,128)S(1)} collective-permute-done((f32[2,64,1536]{2,1,0:T(8,128)S(1)}, f32[2,64,1536]{2,1,0:T(8,128)S(1)}, u32[]{:S(2)}, u32[]{:S(2)}) %collective-permute-start.29) | collective-permute-done | bytes 786464 | tf_op jit(solution)/shard_map/ppermute | solution.py:308
  368.9 31.9 %collective-permute-done.30 = f32[4,64,1536]{2,1,0:T(8,128)} collective-permute-done((f32[4,64,1536]{2,1,0:T(8,128)S(1)}, f32[4,64,1536]{2,1,0:T(8,128)}, u32[]{:S(2)}, u32[]{:S(2)}) %collective-permute-start.30) | collective-permute-done | bytes 1572896 | tf_op jit(solution)/shard_map/ppermute | solution.py:308
  400.8 2.3 maximum_select_fusion
  405.0 9.9 %gram.1 = f32[4,512,512]{2,1,0:T(8,128)} custom-call(f32[512,1536]{1,0:T(8,128)} %bitcast.117), custom_call_target="tpu_custom_call" | custom-call | tf_op jit(solution)/shard_map/gram/pallas_call | solution.py:640
  419.7 6.4 %input_backward.1 = (f32[3,196,512]{2,1,0:T(8,128)}, f32[8,512]{1,0:T(8,128)}) custom-call(s32[1]{0:T(128)} %bitcast.t_ref, bf16[12,196,512]{2,1,0:T(8,128)(2,1)} %tok.5, f32[640,512]{1,0:T(8,128)} %get-tuple-element.44.gmid, bf16[3,4,208,384]{3,2,1,0:T(8,128)(2,1)} %get-tuple-element.49.plow, f32[512,384]{1,0:T(8,128)} %w0.3, f32[512,384]{1,0:T(8,128)} %copy-done.4, ...), custom_call_target="tpu_custom_call" | custom-call | tf_op jit(solution)/shard_map/input_backward/pallas_call | solution.py:562
  430.7 53.0 %collective-permute-done.22 = f32[4516]{0:T(1024)S(1)} collective-permute-done((f32[4516]{0:T(1024)S(1)}, f32[4516]{0:T(1024)S(1)}, u32[]{:S(2)}, u32[]{:S(2)}) %collective-permute-start.22) | collective-permute-done | bytes 18096 | tf_op jit(solution)/shard_map/ppermute | solution.py:304
  483.8 38.1 %psum.7 = f32[4516]{0:T(1024)S(1)} all-reduce(f32[4516]{0:T(1024)S(1)} %fusion.14), channel_id=1, replica_groups=mesh['dp'=8,'tensor'=4] {'dp'}, use_global_device_ids=true, to_apply=%region_0.1 | all-reduce | flops 4516 | bytes 36128 | tf_op jit(solution)/shard_map/psum | solution.py:605
  530.2 9.0 %join_images.3 = f32[12,196,512]{2,1,0:T(8,128)} custom-call(s32[1]{0:T(128)} %bitcast.t_ref, f32[3,196,512]{2,1,0:T(8,128)} %get-tuple-element.50.a0, f32[3,196,512]{2,1,0:T(8,128)} %collective-permute-done.18.a1, f32[3,196,512]{2,1,0:T(8,128)} %collective-permute-done.19.a2, f32[3,196,512]{2,1,0:T(8,128)} %collective-permute-done.20.a3), custom_call_target="tpu_custom_call" | custom-call | tf_op jit(solution)/shard_map/join_images/pallas_call | solution.py:361
  539.3 8.7 %join_images.2 = bf16[12,196,512]{2,1,0:T(8,128)(2,1)} custom-call(s32[1]{0:T(128)} %bitcast.t_ref, f32[3,196,512]{2,1,0:T(8,128)} %get-tuple-element.43.a0, f32[3,196,512]{2,1,0:T(8,128)} %collective-permute-done.15.a1, f32[3,196,512]{2,1,0:T(8,128)} %collective-permute-done.16.a2, f32[3,196,512]{2,1,0:T(8,128)} %collective-permute-done.17.a3), custom_call_target="tpu_custom_call" | custom-call | tf_op jit(solution)/shard_map/join_images/pallas_call | solution.py:361
  549.5 2.3 collective-permute-done.32
  551.8 2.6 fusion.9.g_ref
  554.4 32.6 %newton_schulz.1 = f32[512,512]{1,0:T(8,128)} custom-call(f32[512,512]{1,0:T(8,128)} %fusion.9.g_ref), custom_call_target="tpu_custom_call" | custom-call | tf_op jit(solution)/shard_map/newton_schulz/pallas_call | solution.py:651
  590.3 2.6 collective-permute-done.34
  596.7 4.5 update.1
  (196 shorter events, 79.6 us)
Async XLA Ops:
  0.7 81.6 %collective-permute-start.10 = (f32[512,512]{1,0:T(8,128)}, f32[512,512]{1,0:T(8,128)}, u32[]{:S(2)}, u32[]{:S(2)}) collective-permute-start(f32[512,512]{1,0:T(8,128)} %e0.1), channel_id=1, source_target_pairs={{0,2},{1,3},{2,0},{3,1},{4,6},{5,7},{6,4},{7,5},{8,10},{9,11},{10,... | collective-permute-start | bytes 3145736 | tf_op jit(solution)/shard_map/ppermute | solution.py:304
  3.7 78.9 %collective-permute-start.13 = (f32[512,512]{1,0:T(8,128)}, f32[512,512]{1,0:T(8,128)}, u32[]{:S(2)}, u32[]{:S(2)}) collective-permute-start(f32[512,512]{1,0:T(8,128)} %r0.1), channel_id=1, source_target_pairs={{0,2},{1,3},{2,0},{3,1},{4,6},{5,7},{6,4},{7,5},{8,10},{9,11},{10,... | collective-permute-start | bytes 3145736 | tf_op jit(solution)/shard_map/ppermute | solution.py:304
  3.8 74.5 %collective-permute-start.1 = (f32[512,384]{1,0:T(8,128)}, f32[512,384]{1,0:T(8,128)S(1)}, u32[]{:S(2)}, u32[]{:S(2)}) collective-permute-start(f32[512,384]{1,0:T(8,128)} %w0.3), channel_id=1, source_target_pairs={{0,2},{1,3},{2,0},{3,1},{4,6},{5,7},{6,4},{7,5},{8,10},{9,11},{10,... | collective-permute-start | bytes 2359304 | tf_op jit(solution)/shard_map/ppermute | solution.py:304
  5.8 76.4 %collective-permute-start = (f32[512,384]{1,0:T(8,128)}, f32[512,384]{1,0:T(8,128)S(1)}, u32[]{:S(2)}, u32[]{:S(2)}) collective-permute-start(f32[512,384]{1,0:T(8,128)} %w0.3), channel_id=1, source_target_pairs={{0,1},{1,0},{2,3},{3,2},{4,5},{5,4},{6,7},{7,6},{8,9},{9,8},{10,11... | collective-permute-start | bytes 2359304 | tf_op jit(solution)/shard_map/ppermute | solution.py:304
  7.3 59.3 %collective-permute-start.4 = (f32[2048]{0:T(1024)S(1)}, f32[2048]{0:T(1024)S(1)}, u32[]{:S(2)}, u32[]{:S(2)}) collective-permute-start(f32[2048]{0:T(1024)S(1)} %concatenate.88), channel_id=1, source_target_pairs={{0,2},{1,3},{2,0},{3,1},{4,6},{5,7},{6,4},{7,5},{8,10},{9,11},{10,... | collective-permute-start | bytes 24584 | tf_op jit(solution)/shard_map/ppermute | solution.py:304
  68.9 8.6 %collective-permute-start.7 = (f32[128,512]{1,0:T(8,128)}, f32[128,512]{1,0:T(8,128)S(1)}, u32[]{:S(2)}, u32[]{:S(2)}) collective-permute-start(f32[128,512]{1,0:T(8,128)} %o0.1), channel_id=1, source_target_pairs={{0,2},{1,3},{2,0},{3,1},{4,6},{5,7},{6,4},{7,5},{8,10},{9,11},{10,... | collective-permute-start | bytes 786440 | tf_op jit(solution)/shard_map/ppermute | solution.py:304
  77.5 4.2 collective-permute-start.6
  78.3 6.2 %collective-permute-start.2 = (f32[512,384]{1,0:T(8,128)S(1)}, f32[512,384]{1,0:T(8,128)S(1)}, u32[]{:S(2)}, u32[]{:S(2)}) collective-permute-start(f32[512,384]{1,0:T(8,128)S(1)} %collective-permute-done.1.w2), channel_id=1, source_target_pairs={{0,1},{1,0},{2,3},{3,2},{4,5},{5,4},{6,7},{7,6},{8,9},{9,8},{10,11... | collective-permute-start | bytes 2359304 | tf_op jit(solution)/shard_map/ppermute | solution.py:304
  81.7 25.8 %collective-permute-start.12 = (f32[512,512]{1,0:T(8,128)}, f32[512,512]{1,0:T(8,128)}, u32[]{:S(2)}, u32[]{:S(2)}) collective-permute-start(f32[512,512]{1,0:T(8,128)} %r0.1), channel_id=1, source_target_pairs={{0,1},{1,0},{2,3},{3,2},{4,5},{5,4},{6,7},{7,6},{8,9},{9,8},{10,11... | collective-permute-start | bytes 3145736 | tf_op jit(solution)/shard_map/ppermute | solution.py:304
  82.1 25.4 %collective-permute-start.9 = (f32[512,512]{1,0:T(8,128)}, f32[512,512]{1,0:T(8,128)}, u32[]{:S(2)}, u32[]{:S(2)}) collective-permute-start(f32[512,512]{1,0:T(8,128)} %e0.1), channel_id=1, source_target_pairs={{0,1},{1,0},{2,3},{3,2},{4,5},{5,4},{6,7},{7,6},{8,9},{9,8},{10,11... | collective-permute-start | bytes 3145736 | tf_op jit(solution)/shard_map/ppermute | solution.py:304
  82.3 25.2 %collective-permute-start.11 = (f32[512,512]{1,0:T(8,128)}, f32[512,512]{1,0:T(8,128)}, u32[]{:S(2)}, u32[]{:S(2)}) collective-permute-start(f32[512,512]{1,0:T(8,128)} %collective-permute-done.10.e2), channel_id=1, source_target_pairs={{0,1},{1,0},{2,3},{3,2},{4,5},{5,4},{6,7},{7,6},{8,9},{9,8},{10,11... | collective-permute-start | bytes 3145736 | tf_op jit(solution)/shard_map/ppermute | solution.py:304
  82.7 24.9 %collective-permute-start.14 = (f32[512,512]{1,0:T(8,128)}, f32[512,512]{1,0:T(8,128)}, u32[]{:S(2)}, u32[]{:S(2)}) collective-permute-start(f32[512,512]{1,0:T(8,128)} %collective-permute-done.13.r2), channel_id=1, source_target_pairs={{0,1},{1,0},{2,3},{3,2},{4,5},{5,4},{6,7},{7,6},{8,9},{9,8},{10,11... | collective-permute-start | bytes 3145736 | tf_op jit(solution)/shard_map/ppermute | solution.py:304
  84.5 22.9 %collective-permute-start.8 = (f32[128,512]{1,0:T(8,128)}, f32[128,512]{1,0:T(8,128)}, u32[]{:S(2)}, u32[]{:S(2)}) collective-permute-start(f32[128,512]{1,0:T(8,128)} %copy-done.8), channel_id=1, source_target_pairs={{0,1},{1,0},{2,3},{3,2},{4,5},{5,4},{6,7},{7,6},{8,9},{9,8},{10,11... | collective-permute-start | bytes 786440 | tf_op jit(solution)/shard_map/ppermute | solution.py:304
  161.9 10.2 %collective-permute-start.23 = (f32[2,512,1536]{2,1,0:T(8,128)S(1)}, f32[2,512,1536]{2,1,0:T(8,128)S(1)}, u32[]{:S(2)}, u32[]{:S(2)}) collective-permute-start(f32[2,512,1536]{2,1,0:T(8,128)S(1)} %pad_maximum_fusion), channel_id=1, source_target_pairs={{0,1},{1,0},{2,3},{3,2},{4,5},{5,4},{6,7},{7,6},{8,9},{9,8},{10,11... | collective-permute-start | bytes 18874376 | tf_op jit(solution)/shard_map/ppermute | solution.py:304
  175.8 70.6 %collective-permute-start.24 = (f32[512,1536]{1,0:T(8,128)}, f32[512,1536]{1,0:T(8,128)}, u32[]{:S(2)}, u32[]{:S(2)}) collective-permute-start(f32[512,1536]{1,0:T(8,128)} %fusion), channel_id=1, source_target_pairs={{0,2},{1,3},{2,0},{3,1},{4,6},{5,7},{6,4},{7,5},{8,10},{9,11},{10,... | collective-permute-start | bytes 9437192 | tf_op jit(solution)/shard_map/ppermute | solution.py:304
  251.9 35.9 %collective-permute-start.25 = (f32[4,64,1536]{2,1,0:T(8,128)S(1)}, f32[4,64,1536]{2,1,0:T(8,128)}, u32[]{:S(2)}, u32[]{:S(2)}) collective-permute-start(f32[4,64,1536]{2,1,0:T(8,128)S(1)} %dynamic-slice_bitcast_fusion), channel_id=1, source_target_pairs={{0,4},{4,0},{8,12},{12,8},{16,20},{20,16},{24,28},{28,24},{1,5},{5... | collective-permute-start | bytes 4718600 | tf_op jit(solution)/shard_map/ppermute | solution.py:308
  289.9 18.1 %collective-permute-start.26 = (f32[2,64,1536]{2,1,0:T(8,128)S(1)}, f32[2,64,1536]{2,1,0:T(8,128)}, u32[]{:S(2)}, u32[]{:S(2)}) collective-permute-start(f32[2,64,1536]{2,1,0:T(8,128)S(1)} %dynamic-slice_bitcast_fusion.1), channel_id=1, source_target_pairs={{0,8},{4,12},{8,0},{12,4},{16,24},{20,28},{24,16},{28,20},{1,9},{5... | collective-permute-start | bytes 2359304 | tf_op jit(solution)/shard_map/ppermute | solution.py:308
  309.3 18.0 %collective-permute-start.27 = (f32[1,64,1536]{2,1,0:T(8,128)S(1)}, f32[1,64,1536]{2,1,0:T(8,128)S(1)}, u32[]{:S(2)}, u32[]{:S(2)}) collective-permute-start(f32[1,64,1536]{2,1,0:T(8,128)S(1)} %constant_dynamic-slice_fusion.11), channel_id=1, source_target_pairs={{0,16},{4,20},{8,24},{12,28},{16,0},{20,4},{24,8},{28,12},{1,17},{... | collective-permute-start | bytes 1179656 | tf_op jit(solution)/shard_map/ppermute | solution.py:308
  329.0 19.5 %collective-permute-start.28 = (f32[1,64,1536]{2,1,0:T(8,128)S(1)}, f32[1,64,1536]{2,1,0:T(8,128)S(1)}, u32[]{:S(2)}, u32[]{:S(2)}) collective-permute-start(f32[1,64,1536]{2,1,0:T(8,128)S(1)} %get-tuple-element.90), channel_id=1, source_target_pairs={{0,16},{4,20},{8,24},{12,28},{16,0},{20,4},{24,8},{28,12},{1,17},{... | collective-permute-start | bytes 1179656 | tf_op jit(solution)/shard_map/ppermute | solution.py:308
  348.6 18.0 %collective-permute-start.29 = (f32[2,64,1536]{2,1,0:T(8,128)S(1)}, f32[2,64,1536]{2,1,0:T(8,128)S(1)}, u32[]{:S(2)}, u32[]{:S(2)}) collective-permute-start(f32[2,64,1536]{2,1,0:T(8,128)S(1)} %maximum_select_fusion.3), channel_id=1, source_target_pairs={{0,8},{4,12},{8,0},{12,4},{16,24},{20,28},{24,16},{28,20},{1,9},{5... | collective-permute-start | bytes 2359304 | tf_op jit(solution)/shard_map/ppermute | solution.py:308
  366.7 34.0 %collective-permute-start.30 = (f32[4,64,1536]{2,1,0:T(8,128)S(1)}, f32[4,64,1536]{2,1,0:T(8,128)}, u32[]{:S(2)}, u32[]{:S(2)}) collective-permute-start(f32[4,64,1536]{2,1,0:T(8,128)S(1)} %bitcast.123), channel_id=1, source_target_pairs={{0,4},{4,0},{8,12},{12,8},{16,20},{20,16},{24,28},{28,24},{1,5},{5... | collective-permute-start | bytes 4718600 | tf_op jit(solution)/shard_map/ppermute | solution.py:308
  418.3 106.8 %collective-permute-start.31 = (f32[2,512,512]{2,1,0:T(8,128)}, f32[2,512,512]{2,1,0:T(8,128)S(1)}, u32[]{:S(2)}, u32[]{:S(2)}) collective-permute-start(f32[2,512,512]{2,1,0:T(8,128)} %pad_maximum_fusion.1), channel_id=1, source_target_pairs={{0,1},{1,0},{2,3},{3,2},{4,5},{5,4},{6,7},{7,6},{8,9},{9,8},{10,11... | collective-permute-start | bytes 6291464 | tf_op jit(solution)/shard_map/ppermute | solution.py:304
  427.7 94.2 %collective-permute-start.19 = (f32[3,196,512]{2,1,0:T(8,128)}, f32[3,196,512]{2,1,0:T(8,128)}, u32[]{:S(2)}, u32[]{:S(2)}) collective-permute-start(f32[3,196,512]{2,1,0:T(8,128)} %get-tuple-element.50.a0), channel_id=1, source_target_pairs={{0,2},{1,3},{2,0},{3,1},{4,6},{5,7},{6,4},{7,5},{8,10},{9,11},{10,... | collective-permute-start | bytes 3612680 | tf_op jit(solution)/shard_map/ppermute | solution.py:304
  428.5 93.5 %collective-permute-start.16 = (f32[3,196,512]{2,1,0:T(8,128)}, f32[3,196,512]{2,1,0:T(8,128)}, u32[]{:S(2)}, u32[]{:S(2)}) collective-permute-start(f32[3,196,512]{2,1,0:T(8,128)} %get-tuple-element.43.a0), channel_id=1, source_target_pairs={{0,2},{1,3},{2,0},{3,1},{4,6},{5,7},{6,4},{7,5},{8,10},{9,11},{10,... | collective-permute-start | bytes 3612680 | tf_op jit(solution)/shard_map/ppermute | solution.py:304
  430.0 53.7 %collective-permute-start.22 = (f32[4516]{0:T(1024)S(1)}, f32[4516]{0:T(1024)S(1)}, u32[]{:S(2)}, u32[]{:S(2)}) collective-permute-start(f32[4516]{0:T(1024)S(1)} %pad_maximum_fusion.4), channel_id=1, source_target_pairs={{0,2},{1,3},{2,0},{3,1},{4,6},{5,7},{6,4},{7,5},{8,10},{9,11},{10,... | collective-permute-start | bytes 54200 | tf_op jit(solution)/shard_map/ppermute | solution.py:304
  430.7 99.5 %collective-permute-start.18 = (f32[3,196,512]{2,1,0:T(8,128)}, f32[3,196,512]{2,1,0:T(8,128)}, u32[]{:S(2)}, u32[]{:S(2)}) collective-permute-start(f32[3,196,512]{2,1,0:T(8,128)} %get-tuple-element.50.a0), channel_id=1, source_target_pairs={{0,1},{1,0},{2,3},{3,2},{4,5},{5,4},{6,7},{7,6},{8,9},{9,8},{10,11... | collective-permute-start | bytes 3612680 | tf_op jit(solution)/shard_map/ppermute | solution.py:304
  483.7 55.6 %collective-permute-start.15 = (f32[3,196,512]{2,1,0:T(8,128)}, f32[3,196,512]{2,1,0:T(8,128)}, u32[]{:S(2)}, u32[]{:S(2)}) collective-permute-start(f32[3,196,512]{2,1,0:T(8,128)} %get-tuple-element.43.a0), channel_id=1, source_target_pairs={{0,1},{1,0},{2,3},{3,2},{4,5},{5,4},{6,7},{7,6},{8,9},{9,8},{10,11... | collective-permute-start | bytes 3612680 | tf_op jit(solution)/shard_map/ppermute | solution.py:304
  522.0 8.3 %collective-permute-start.20 = (f32[3,196,512]{2,1,0:T(8,128)}, f32[3,196,512]{2,1,0:T(8,128)}, u32[]{:S(2)}, u32[]{:S(2)}) collective-permute-start(f32[3,196,512]{2,1,0:T(8,128)} %collective-permute-done.19.a2), channel_id=1, source_target_pairs={{0,1},{1,0},{2,3},{3,2},{4,5},{5,4},{6,7},{7,6},{8,9},{9,8},{10,11... | collective-permute-start | bytes 3612680 | tf_op jit(solution)/shard_map/ppermute | solution.py:304
  522.0 17.3 %collective-permute-start.17 = (f32[3,196,512]{2,1,0:T(8,128)}, f32[3,196,512]{2,1,0:T(8,128)}, u32[]{:S(2)}, u32[]{:S(2)}) collective-permute-start(f32[3,196,512]{2,1,0:T(8,128)} %collective-permute-done.16.a2), channel_id=1, source_target_pairs={{0,1},{1,0},{2,3},{3,2},{4,5},{5,4},{6,7},{7,6},{8,9},{9,8},{10,11... | collective-permute-start | bytes 3612680 | tf_op jit(solution)/shard_map/ppermute | solution.py:304
  526.6 25.2 %collective-permute-start.32 = (f32[512,512]{1,0:T(8,128)S(1)}, f32[512,512]{1,0:T(8,128)S(1)}, u32[]{:S(2)}, u32[]{:S(2)}) collective-permute-start(f32[512,512]{1,0:T(8,128)S(1)} %fusion.7), channel_id=1, source_target_pairs={{0,2},{1,3},{2,0},{3,1},{4,6},{5,7},{6,4},{7,5},{8,10},{9,11},{10,... | collective-permute-start | bytes 3145736 | tf_op jit(solution)/shard_map/ppermute | solution.py:304
  587.9 5.0 collective-permute-start.34
  590.3 5.4 collective-permute-start.33
  (23 other events, 909.9 us)
